TPU v7x, 512 devices: a whole 4x8x8 slice. The times are simulated.
512 devices in a mesh: prow: 16 (over y, x_lo), pcol: 32 (over x_hi, z, core).
Axes of the slice: x: 4 (x_hi: 2, x_lo: 2; x = x_hi * 2 + x_lo), y: 8, z: 8, core: 2. Of those that a mesh axis runs over, the one named last changes fastest.
Arguments:
- matrix: float32 [12288, 12288], P('prow', 'pcol'), may hold values from -6 to 6, as said below
- reflectors: float32 [12288, 512], P('prow'), may hold values from -0.0546875 to 0.0546875
- factors: float32 [2, 256, 256], replicated, may hold values from -0.25 to 2, as said below
Outputs:
- updated: float32 [12288, 12288], P('prow', 'pcol')
Inputs may be any that keep to these rules, and one draw needn't show every extreme that they name: `matrix`: symmetric: entry (i, j) equals entry (j, i). `factors`: each of the 2 blocks is upper triangular with diagonal entries between 1 and 2.
All inputs are finite; a program needn't handle non-finite values.
Results may differ from a plain program's by a relative error of at most 0.0001.
Values sent between devices are 32-bit elements; how exact they have to be, the bound alone decides.
A program may use at most 64 MiB of HBM per device.

v0:
```python
import jax
import jax.numpy as jnp
from jax import lax
from jax.sharding import PartitionSpec as P


def spread(block, axis, owner):
    block = jnp.where(lax.axis_index(axis) == owner, block, jnp.zeros_like(block))
    return lax.psum(block, axis)


def high_dot(left, right):
    return jnp.dot(left, right, precision=lax.Precision.HIGHEST, preferred_element_type=jnp.float32)


def inner_dot(left, right):
    return lax.dot_general(
        left,
        right,
        (((0,), (0,)), ((), ())),
        precision=lax.Precision.HIGHEST,
        preferred_element_type=jnp.float32,
    )


def outer_dot(left, right):
    return lax.dot_general(
        left,
        right,
        (((1,), (1,)), ((), ())),
        precision=lax.Precision.HIGHEST,
        preferred_element_type=jnp.float32,
    )


def body(matrix, reflectors, factors):
    row_count, col_count = matrix.shape
    panel_width = factors.shape[1]
    panel_count = factors.shape[0]
    col_ratio = lax.axis_size("pcol") // lax.axis_size("prow")
    col_index = lax.axis_index("pcol")
    owner_rows = lax.dynamic_slice_in_dim(
        reflectors, col_index % col_ratio * col_count, col_count, 0
    )
    column_reflectors = spread(owner_rows, "prow", col_index // col_ratio)
    current = matrix
    for panel in range(panel_count):
        row_vectors = reflectors[:, panel * panel_width : (panel + 1) * panel_width]
        column_vectors = column_reflectors[:, panel * panel_width : (panel + 1) * panel_width]
        factor = factors[panel]
        row_sums = lax.psum(high_dot(current, column_vectors), "pcol")
        own_block = lax.dynamic_slice_in_dim(
            row_sums, col_index % col_ratio * col_count, col_count, 0
        )
        column_sums = spread(own_block, "prow", col_index // col_ratio)
        row_sums, column_sums = (row_sums, column_sums)
        row_proj = high_dot(row_sums, factor)
        column_proj = high_dot(column_sums, factor)
        gram = lax.psum(inner_dot(row_vectors, row_proj), "prow")
        coupling = inner_dot(factor, gram)
        row_fixed = row_proj - 0.5 * high_dot(row_vectors, coupling)
        column_fixed = column_proj - 0.5 * high_dot(column_vectors, coupling)
        current = (
            current - outer_dot(row_vectors, column_fixed) - outer_dot(row_fixed, column_vectors)
        )
    return current


def solution(mesh):
    return jax.shard_map(
        body,
        mesh=mesh,
        in_specs=(P("prow", "pcol"), P("prow", None), P()),
        out_specs=P("prow", "pcol"),
        check_vma=False,
    )
```

profile of v0, /device:TPU:1, one launch (start us, length us, event | category | flops | bytes accessed | tf_op | source)
XLA Modules:
  0.0 1022.3 jit_solution(7563614646533199371)
XLA Ops:
  6.5 2.2 dynamic-slice_select_fusion
  8.8 140.4 %all-reduce.8.cloned.1.call-done = f32[384,512]{1,0:T(8,128)} async-done(((f32[384,512]{1,0:T(8,128)}), f32[384,512]{1,0:T(8,128)}) %all-reduce.8.cloned.1.call-update) | async-done | bytes 786448 | tf_op jit(solution)/shard_map/psum | solution.py:9
  149.2 3.9 convolution_bitcast_fusion.2
  153.2 284.4 %all-reduce.10.cloned.1.call-done = f32[768,256]{0,1:T(8,128)} async-done(((f32[768,256]{0,1:T(8,128)}), f32[768,256]{0,1:T(8,128)}) %all-reduce.10.cloned.1.call-update) | async-done | bytes 786448 | tf_op jit(solution)/shard_map/psum | solution.py:51
  437.6 2.5 fusion.30
  440.1 2.1 convolution_bitcast_fusion.4
  443.3 2.7 copy.4
  445.9 128.2 %all-reduce.16.cloned.1.call-done = (f32[256,256]{0,1:T(8,128)}, f32[384,256]{0,1:T(8,128)}) async-done(((f32[256,256]{0,1:T(8,128)}, f32[384,256]{0,1:T(8,128)}), (f32[256,256]{0,1:T(8,128)}, f32[384,256]{0,1:T(8,128)})) %all-reduce.16.cloned.1.call-update) | async-done | bytes 655376 | tf_op jit(solution)/shard_map/psum | solution.py:59
  574.2 1.3 fusion.28
  575.5 0.8 fusion.7
  577.8 0.8 convolution_subtract_fusion.1
  578.6 1.2 fusion.19
  579.9 1.2 fusion.1
  581.0 2.4 fusion.17
  583.7 284.2 %all-reduce.12.cloned.1.call-done = f32[768,256]{0,1:T(8,128)} async-done(((f32[768,256]{0,1:T(8,128)}), f32[768,256]{0,1:T(8,128)}) %all-reduce.12.cloned.1.call-update) | async-done | bytes 786448 | tf_op jit(solution)/shard_map/psum | solution.py:51
  867.9 2.6 fusion.25
  870.5 0.9 copy-done.2
  871.4 2.1 convolution_bitcast_fusion.3
  874.3 131.2 %all-reduce.14.cloned.1.call-done = (f32[256,256]{0,1:T(8,128)}, f32[384,256]{0,1:T(8,128)}) async-done(((f32[256,256]{0,1:T(8,128)}, f32[384,256]{0,1:T(8,128)}), (f32[256,256]{0,1:T(8,128)}, f32[384,256]{0,1:T(8,128)})) %all-reduce.14.cloned.1.call-update) | async-done | bytes 655376 | tf_op jit(solution)/shard_map/psum | solution.py:59
  1005.5 1.5 fusion.23
  1007.0 0.8 fusion.5
  1009.8 1.2 fusion.14
  1010.9 2.2 fusion.3
  1013.1 2.7 copy.8
  (40 shorter events, 5.7 us)
Async XLA Ops:
  6.5 142.6 %all-reduce.8.cloned.1.call-start = ((), (), s32[]{:S(2)}) async-start(), calls=%async_computation | async-start | bytes 1572864 | tf_op jit(solution)/shard_map/psum | solution.py:9
  6.5 142.6 %copy-start.7 = (f32[768,384]{1,0:T(8,128)S(1)}, f32[768,384]{1,0:T(8,128)}, u32[]{:S(2)}) copy-start(f32[768,384]{1,0:T(8,128)} %param.3) | copy-start | bytes 3538948
  8.7 428.8 %copy-start.4 = (f32[2,256,256]{2,1,0:T(8,128)S(1)}, f32[2,256,256]{2,1,0:T(8,128)}, u32[]{:S(2)}) copy-start(f32[2,256,256]{2,1,0:T(8,128)} %param.5) | copy-start | bytes 1572868
  8.7 428.8 %all-reduce.10.cloned.1.call-start = ((), (), s32[]{:S(2)}) async-start(), calls=%async_computation.1 | async-start | bytes 1572864 | tf_op jit(solution)/shard_map/psum | solution.py:51
  153.1 287.0 %copy-start = (f32[768,512]{1,0:T(8,128)S(1)}, f32[768,512]{1,0:T(8,128)}, u32[]{:S(2)}) copy-start(f32[768,512]{1,0:T(8,128)} %param.4) | copy-start | bytes 4718596
  153.1 421.0 %all-reduce.16.cloned.1.call-start = ((), (), s32[]{:S(2)}) async-start(), calls=%async_computation.4 | async-start | bytes 1310720 | tf_op jit(solution)/shard_map/psum | solution.py:59
  440.1 2.1 copy-start.10
  443.1 424.9 %all-reduce.12.cloned.1.call-start = ((), (), s32[]{:S(2)}) async-start(), calls=%async_computation.2 | async-start | bytes 1572864 | tf_op jit(solution)/shard_map/psum | solution.py:51
  575.5 1.1 copy-start.1
  576.6 1.0 copy-start.5
  576.6 1.2 copy-start.11
  578.6 1.3 copy-start.8
  583.4 422.1 %all-reduce.14.cloned.1.call-start = ((), (), s32[]{:S(2)}) async-start(), calls=%async_computation.3 | async-start | bytes 1310720 | tf_op jit(solution)/shard_map/psum | solution.py:59
  870.5 0.9 copy-start.2
  871.4 2.1 copy-start.9
  1005.5 1.5 copy-start.3
  1007.8 1.0 copy-start.6
  1007.8 1.1 copy-start.12
Sparse Core Ops, SparseCore 0:
  10.3 138.8 all-reduce.7
  153.2 284.2 all-reduce.9
  443.2 130.9 all-reduce.15
  583.5 284.3 all-reduce.11
  874.4 130.9 all-reduce.13
where the time goes:
time: 1030 us; the launch traced here: 1020 us
  waiting for transfers between devices  968 us (94%)
  matrix products  28.4 us (3%)
  between operations  13.3 us (1%)
    psum x2, waiting for transfers between devices, body(): row_sums = lax.psum(high_dot(current, column_vectors), 'pcol')  569 us
    psum x2, waiting for transfers between devices, body(): gram = lax.psum(inner_dot(row_vectors, row_proj), 'prow')  259 us
    psum x1, waiting for transfers between devices, spread(): return lax.psum(block, axis)  140 us
  transfers between devices with their start and end apart: 5, of which 5 were waited for; matrix products, arithmetic and copies ran while one was open for 0% of the time, Pallas kernels for 0%

commit v1 on v0

v1 whole, which is shorter than its diff:
```python
import jax
import jax.numpy as jnp
from jax import lax
from jax.experimental import pallas as pl
from jax.experimental.pallas import tpu as pltpu
from jax.sharding import PartitionSpec as P

F32 = jnp.float32
BF16 = jnp.bfloat16
RING = 8
NN = (((1,), (0,)), ((), ()))
TN = (((0,), (0,)), ((), ()))
NT = (((1,), (1,)), ((), ()))


def split(x):
    high = x.astype(BF16)
    return high, (x - high.astype(F32)).astype(BF16)


def dot3(left, right, dims):
    (lh, ll), (rh, rl) = left, right
    def one(p, q):
        return lax.dot_general(p, q, dims, preferred_element_type=F32)
    return one(lh, rh) + (one(lh, rl) + one(ll, rh))


def mm(left, right, dims):
    return dot3(split(left), split(right), dims)


def kernel(a_ref, v_ref, t_ref, upd_ref, vh, vl, pt, rs_recv, zx_recv, zcol, vcol, zrow, s21, gloc,
           ga_recv, gb_recv, gtiles, gc_recv, gfull, qh, ql, uh, ul, yt1_ref, send_sems, recv_sems):
    rows, width = v_ref.shape
    cols = a_ref.shape[1]
    nb = width // 2
    sub = width // 16
    vsub = cols // 16
    r = lax.axis_index("prow")
    c = lax.axis_index("pcol")
    y, xl = r // 2, r % 2
    chip, k = c // 2, c % 2
    xh, z = chip // 8, chip % 8

    y_up, y_down = ((y + 1) % RING * 2 + xl, c), ((y + RING - 1) % RING * 2 + xl, c)
    z_up = (r, (xh * 8 + (z + 1) % RING) * 2 + k)
    z_down = (r, (xh * 8 + (z + RING - 1) % RING) * 2 + k)
    x_near = (y * 2 + 1 - xl, c)
    x_far = (r, ((1 - xh) * 8 + z) * 2 + k)
    other = (r, chip * 2 + 1 - k)
    mirror = (chip, r * 2 + k)
    apart = r != chip

    count = [0]
    started = []

    def copy(src, dst, device):
        slot = count[0]
        count[0] += 1
        return pltpu.make_async_remote_copy(
            src_ref=src, dst_ref=dst, send_sem=send_sems.at[slot], recv_sem=recv_sems.at[slot],
            device_id=device, device_id_type=pl.DeviceIdType.MESH)

    def go(op):
        op.start()
        started.append(op)
        return op

    barrier = pltpu.get_barrier_semaphore()
    y_peers = [((y + o) % RING * 2 + xl, c) for o in range(1, RING)]
    fixed = [*y_peers, x_near, z_up, z_down, x_far, other]
    for device in fixed:
        pl.semaphore_signal(barrier, inc=1, device_id=device, device_id_type=pl.DeviceIdType.MESH)

    @pl.when(apart)
    def _():
        pl.semaphore_signal(barrier, inc=1, device_id=mirror, device_id_type=pl.DeviceIdType.MESH)

    high, low = split(v_ref[...])
    vh[...] = high
    vl[...] = low
    a_split = split(a_ref[...])
    for j in range(width // 128):
        lanes = slice(j * 128, (j + 1) * 128)
        pt[lanes, :] = dot3((vh[:, lanes], vl[:, lanes]), a_split, TN)

    pl.semaphore_wait(barrier, len(fixed) + apart.astype(jnp.int32))

    v_out = v_ref.at[pl.ds(pl.multiple_of(k * cols + chip // 2 * 2 * vsub, 8), 2 * vsub), :]
    v_to = vcol.at[pl.ds(pl.multiple_of(chip // 2 * 2 * vsub, 8), 2 * vsub), :]
    v_copy = copy(v_out, v_to, mirror)

    def pt_at(half, index):
        return pl.ds(pl.multiple_of((index + RING) % RING * (2 * sub) + half * sub, sub), sub)

    def rs_op(name, s):
        right = name[0] == "R"
        half = 0 if name[1] == "A" else 1
        index = y + 4 - s if right else y - 4 + s
        slot = {"RA": 0, "LB": 4, "RB": 8 - 1, "LA": 11 - 1}[name] + s
        return copy(pt.at[pt_at(half, index), :], rs_recv.at[slot], y_up if right else y_down), slot

    first = {"RA": 0, "LB": 0, "RB": 1, "LA": 1}
    rs = {}
    for name in ("RA", "LB", "RB", "LA"):
        rs[name, first[name]] = rs_op(name, first[name])
        go(rs[name, first[name]][0])

    @pl.when(apart)
    def _():
        v_copy.start()

    @pl.when(jnp.logical_not(apart))
    def _():
        vcol[pl.ds(pl.multiple_of(chip // 2 * 2 * vsub, 8), 2 * vsub), :] = (
            v_ref[pl.ds(pl.multiple_of(k * cols + chip // 2 * 2 * vsub, 8), 2 * vsub), :])

    half_rows = pl.ds(pl.multiple_of(k * cols, 128), cols)
    s21[...] = dot3((vh[half_rows, nb:], vl[half_rows, nb:]), (vh[half_rows, :nb], vl[half_rows, :nb]), TN)

    for s in range(1, 4):
        for name in ("RA", "LB", "RB", "LA"):
            if s - 1 < first[name]:
                continue
            op, slot = rs[name, s - 1]
            op.wait_recv()
            half = 0 if name[1] == "A" else 1
            index = y + 4 - s if name[0] == "R" else y - 4 + s
            at = pt_at(half, index)
            pt[at, :] = pt[at, :] + rs_recv[slot]
            rs[name, s] = rs_op(name, s)
            go(rs[name, s][0])
    for half, names in ((0, ("RA", "LA")), (1, ("LB", "RB"))):
        at = pt_at(half, y)
        total = pt[at, :]
        for name in names:
            op, slot = rs[name, 3]
            op.wait_recv()
            total = total + rs_recv[slot]
        pt[at, :] = total

    x_ops = []
    for which in range(2):
        half = (1 - xl) if which == 0 else xl
        x_ops.append(go(copy(pt.at[pt_at(half, y), :], zx_recv.at[pl.ds(pl.multiple_of(half * sub, sub), sub), :], x_near)))

    @pl.when(apart)
    def _():
        v_copy.wait_recv()

    def ring(ref_of, me, up, down):
        ops = {}
        def start(name, s):
            right = name[0] == "R"
            index = (me - s + RING) % RING if right else (me + s) % RING
            ref = ref_of(0 if name[1] == "A" else 1, index)
            ops[name, s] = go(copy(ref, ref, up if right else down))
        last = {"RA": 3, "LB": 3, "RB": 2, "LA": 2}
        def step(s, arrived=None):
            for name in ("RA", "LB", "RB", "LA"):
                if s >= 1 and s - 1 <= last[name]:
                    ops[name, s - 1].wait_recv()
                if s <= last[name]:
                    start(name, s)
                if arrived is not None and s >= 1 and s - 1 <= last[name]:
                    index = (me - s + RING) % RING if name[0] == "R" else (me + s) % RING
                    arrived(0 if name[1] == "A" else 1, index)
        return step

    v_ring = ring(lambda h, i: vcol.at[pl.ds(pl.multiple_of(i * 2 * vsub + h * vsub, 8), vsub), :], y, y_up, y_down)
    z_ring = ring(lambda h, i: zcol.at[pt_at(h, i), :], y, y_up, y_down)

    def zrow_at(core, h, i):
        return zrow.at[core, pl.ds(pl.multiple_of((h * 8 + i) * sub, sub), sub), :]

    row_ring = ring(lambda h, i: zrow_at(k, h, i), z, z_up, z_down)
    g_ring = ring(lambda h, i: gfull.at[(h * 8 + i) * 2 + k], z, z_up, z_down)
    to_other = []

    def pass_row(h, i):
        to_other.append(go(copy(zrow_at(k, h, i), zrow_at(k, h, i), other)))

    def pass_g(h, i):
        ref = gfull.at[(h * 8 + i) * 2 + k]
        to_other.append(go(copy(ref, ref, other)))

    own = pt_at(xl, y)
    x_ops[0].wait_recv()
    zcol[own, :] = pt[own, :] + zx_recv[pl.ds(pl.multiple_of(xl * sub, sub), sub), :]
    row_to = zrow.at[k, pl.ds(pl.multiple_of(r * sub, sub), sub), :]
    z_copy = copy(zcol.at[own, :], row_to, mirror)

    @pl.when(apart)
    def _():
        z_copy.start()

    @pl.when(jnp.logical_not(apart))
    def _():
        zrow[k, pl.ds(pl.multiple_of(r * sub, sub), sub), :] = zcol[own, :]

    x_ops[1].wait_recv()
    rest = pt_at(1 - xl, y)
    zcol[rest, :] = pt[rest, :] + zx_recv[pl.ds(pl.multiple_of((1 - xl) * sub, sub), sub), :]
    z_ring(0)
    v_ring(0)

    @pl.when(apart)
    def _():
        z_copy.wait_recv()

    mine = zrow_at(k, xh, z)
    far_op = go(copy(mine, mine, x_far))
    slice_rows = pl.ds(pl.multiple_of(chip * sub, sub), sub)
    part = dot3(split(zrow[k, slice_rows, :]), (vh[half_rows, :], vl[half_rows, :]), NN)
    late = chip >= 8
    s_rows = s21[pl.ds(pl.multiple_of(chip % 8 * sub, sub), sub), :]
    gloc[:, :nb] = jnp.where(late, s_rows, part[:, :nb])
    gloc[:, nb:] = part[:, nb:]
    half = sub // 2
    ga = go(copy(gloc.at[pl.ds(pl.multiple_of((1 - k) * half, half), half), :], ga_recv, other))
    pass_row(xh, z)
    z_ring(1)
    ga.wait_recv()
    my_half = pl.ds(pl.multiple_of(k * half, half), half)
    gloc[my_half, :] = gloc[my_half, :] + ga_recv[...]
    gb = go(copy(gloc.at[my_half, :], gb_recv, x_near))
    far_op.wait_recv()
    row_ring(0)
    pass_row(1 - xh, z)
    v_ring(1)
    gb.wait_recv()
    total = gloc[my_half, :] + gb_recv[...]
    for j in range(8):
        gtiles[j] = total[j // 4 * 8:j // 4 * 8 + 8, j % 4 * 128:(j % 4 + 1) * 128]
    gc = [go(copy(gtiles.at[(y + o) % RING], gc_recv.at[o], y_peers[o - 1])) for o in range(1, RING)]
    row_ring(1, pass_row)
    z_ring(2)
    tile = gtiles[y]
    for o in range(1, RING):
        gc[o - 1].wait_recv()
        tile = tile + gc_recv[o]
    gfull[c, y] = tile
    gd = [go(copy(gfull.at[c, y], gfull.at[c, y], y_peers[o - 1])) for o in range(1, RING)]
    v_ring(2)
    row_ring(2, pass_row)
    for op in gd:
        op.wait_recv()
    ge = go(copy(gfull.at[c], gfull.at[c], x_far))
    pass_g(xh, z)
    z_ring(3)
    v_ring(3)
    ge.wait_recv()
    g_ring(0)
    pass_g(1 - xh, z)
    row_ring(3, pass_row)
    z_ring(4)
    g_ring(1, pass_g)
    v_ring(4)
    row_ring(4, pass_row)
    g_ring(2, pass_g)

    t1, t2 = split(t_ref[0]), split(t_ref[1])
    yt1 = dot3(t1, split(zcol[:nb, :]), TN)
    yt1_ref[...] = yt1
    qh[:nb, :], ql[:nb, :] = split(yt1)
    qh[nb:, :], ql[nb:, :] = split(dot3(t2, split(zcol[nb:, :]), TN))
    g_ring(3, pass_g)
    v1, v2 = split(vcol[:, :nb]), split(vcol[:, nb:])
    uh[:nb, :], ul[:nb, :] = split(dot3(t1, v1, NT))
    uh[nb:, :], ul[nb:, :] = split(dot3(t2, v2, NT))
    g_ring(4, pass_g)
    for op in to_other:
        op.wait_recv()

    def sweep(depth, first_pass):
        for h in range(2):
            def body(i, _, h=h):
                at = pl.ds(pl.multiple_of(h * cols + i * 128, 128), 128)
                lanes = pl.ds(pl.multiple_of(i * 128, 128), 128)
                acc = dot3((vh[at, :], vl[at, :]), (qh[...], ql[...]), NN)
                acc = acc + dot3(split(zrow[h, :depth, lanes]), (uh[:depth, :], ul[:depth, :]), TN)
                upd_ref[at, :] = -acc if first_pass else upd_ref[at, :] - acc
                return 0
            lax.fori_loop(0, cols // 128, body, 0)

    sweep(width, True)


    def block(row, col):
        parts = []
        for lane in range(2):
            j = col * 2 + lane
            both = [gfull[row * 16:(row + 1) * 16, h * 4 + j] for h in range(2)]
            parts.append(jnp.stack(both, axis=1).reshape(nb, 128))
        return jnp.concatenate(parts, axis=1)

    g11, g12, s_21, g22 = block(0, 0), block(0, 1), block(1, 0), block(1, 1)
    s_21s = split(s_21)
    s_12 = s_21.T
    s_12s = split(s_12)
    e = dot3(s_12s, t2, NN)
    es = split(e)
    m1 = dot3(t1, split(dot3(split(g11), t1, NN)), TN)
    m1s = split(m1)
    kk = dot3(t1, split(g12), TN) - 0.5 * dot3(m1s, s_12s, TN)
    kks = split(kk)
    jj = dot3(s_21s, kks, NN)
    m2 = dot3(t2, split(dot3(split(g22 - jj - jj.T), t2, NN)), TN)
    h12s = split(0.5 * dot3(m1s, es, NN) - dot3(kks, t2, NN))
    qh[:nb, :], ql[:nb, :] = split(dot3(h12s, v2, NT) - dot3(m1s, v1, NT))
    low_q = dot3(h12s, v1, (((0,), (1,)), ((), ()))) - dot3(split(m2), v2, NT)
    qh[nb:, :], ql[nb:, :] = split(low_q - dot3(es, split(yt1_ref[...]), TN))
    uh[:nb, :], ul[:nb, :] = split(-dot3(t1, split(dot3(es, v2, NT)), NN))
    sweep(nb, False)

    for op in started:
        op.wait_send()

    @pl.when(apart)
    def _():
        v_copy.wait_send()
        z_copy.wait_send()


COPIES = 14 + 2 + 2 + 14 + 14 + (1 + 14 + 16) + (1 + 1 + 7 + 7 + 1 + 14 + 16)


def body(matrix, reflectors, factors):
    rows, cols = matrix.shape
    width = reflectors.shape[1]
    nb = width // 2
    sub = width // 16
    vmem = pl.BlockSpec(memory_space=pltpu.VMEM)
    update = pl.pallas_call(
        kernel,
        out_shape=jax.ShapeDtypeStruct((rows, cols), F32),
        in_specs=[vmem] * 3,
        out_specs=vmem,
        scratch_shapes=[
            pltpu.VMEM((rows, width), BF16),
            pltpu.VMEM((rows, width), BF16),
            pltpu.VMEM((width, cols), F32),
            pltpu.VMEM((14, sub, cols), F32),
            pltpu.VMEM((2 * sub, cols), F32),
            pltpu.VMEM((width, cols), F32),
            pltpu.VMEM((cols, width), F32),
            pltpu.VMEM((2, width, cols), F32),
            pltpu.VMEM((nb, nb), F32),
            pltpu.VMEM((sub, width), F32),
            pltpu.VMEM((sub // 2, width), F32),
            pltpu.VMEM((sub // 2, width), F32),
            pltpu.VMEM((8, 8, 128), F32),
            pltpu.VMEM((8, 8, 128), F32),
            pltpu.VMEM((32, 8, 8, 128), F32),
            pltpu.VMEM((width, cols), BF16),
            pltpu.VMEM((width, cols), BF16),
            pltpu.VMEM((width, cols), BF16),
            pltpu.VMEM((width, cols), BF16),
            pltpu.VMEM((nb, cols), F32),
            pltpu.SemaphoreType.DMA((COPIES,)),
            pltpu.SemaphoreType.DMA((COPIES,)),
        ],
        compiler_params=pltpu.CompilerParams(
            collective_id=0, has_side_effects=True, vmem_limit_bytes=48 * 1024 * 1024),
        name="two_panels",
    )(matrix, reflectors, factors)
    return matrix + update


def solution(mesh):
    return jax.shard_map(
        body,
        mesh=mesh,
        in_specs=(P("prow", "pcol"), P("prow", None), P()),
        out_specs=P("prow", "pcol"),
        check_vma=False,
    )
```

time: 1030 us -> 102 us (0.10)
  waiting for transfers between devices: 968 us -> 0 us
  Pallas kernels: 0 us -> 97.4 us
  matrix products: 28.4 us -> 0 us
  between operations: 13.3 us -> 0.01 us
    psum x5 -> x0, waiting for transfers between devices: 968 us -> none  [the longest x2 569 us: body(): row_sums = lax.psum(high_dot(current, column_vectors), 'pcol')]
    pallas_call x0 -> x1, Pallas kernels: none -> 97.4 us  [body(): pl.pallas_call(kernel, out_shape=jax.ShapeDtypeStruct((rows, cols), F32),...]
    dot_general x18 -> x0, matrix products: 28.4 us -> none  [the longest x10 15.7 us: high_dot(): jnp.dot(left, right, precision=lax.Precision.HIGHEST, preferred_element_t...]
  transfers between devices with their start and end apart: 5 -> 0, of which waited for: 5 -> 0; matrix products, arithmetic and copies ran while one was open for 0% -> 0% of each run, Pallas kernels for 0% -> 0%
where the time goes in v1:
time: 102 us
  Pallas kernels  97.4 us (95%)
  local copies, waits for them, and re-layouts  3.72 us (4%)
  other arithmetic  1.13 us (1%)
    pallas_call x1, Pallas kernels, body(): pl.pallas_call(kernel, out_shape=jax.ShapeDtypeStruct((rows, cols), F32),...  97.4 us
    unnamed x6, local copies, waits for them, and re-layouts  3.72 us

profile of v1, /device:TPU:1, one launch (start us, length us, event | category | flops | bytes accessed | tf_op | source)
XLA Modules:
  0.0 102.3 jit_solution(5211052542779344265)
XLA Ops:
  0.0 0.0 copy-start
  0.0 1.3 %copy-done = f32[768,384]{1,0:T(8,128)S(1)} copy-done((f32[768,384]{1,0:T(8,128)S(1)}, f32[768,384]{1,0:T(8,128)}, u32[]{:S(2)}) %copy-start) | copy-done | bytes 1179672
  1.3 0.0 copy-start.1
  1.3 1.4 %copy-done.1 = f32[768,512]{1,0:T(8,128)S(1)} copy-done((f32[768,512]{1,0:T(8,128)S(1)}, f32[768,512]{1,0:T(8,128)}, u32[]{:S(2)}) %copy-start.1) | copy-done | bytes 1572888
  2.7 0.0 copy-start.2
  2.7 1.0 %copy-done.2 = f32[2,256,256]{2,1,0:T(8,128)S(1)} copy-done((f32[2,256,256]{2,1,0:T(8,128)S(1)}, f32[2,256,256]{2,1,0:T(8,128)}, u32[]{:S(2)}) %copy-start.2) | copy-done | bytes 524312
  3.7 97.4 %two_panels.1 = f32[768,384]{1,0:T(8,128)S(1)} custom-call(f32[768,384]{1,0:T(8,128)S(1)} %copy-done, f32[768,512]{1,0:T(8,128)S(1)} %copy-done.1, f32[2,256,256]{2,1,0:T(8,128)S(1)} %copy-done.2), custom_call_target="tpu_custom_call" | custom-call | tf_op jit(solution)/shard_map/two_panels/pallas_call | solution.py:334
  101.1 1.1 %add.3 = f32[768,384]{1,0:T(8,128)} add(f32[768,384]{1,0:T(8,128)S(1)} %copy-done, f32[768,384]{1,0:T(8,128)S(1)} %two_panels.1) | non-fusion elementwise | flops 294912 | bytes 3538944 | tf_op jit(solution)/shard_map/add | solution.py:367
Async XLA Ops:
  0.0 1.3 %copy-start = (f32[768,384]{1,0:T(8,128)S(1)}, f32[768,384]{1,0:T(8,128)}, u32[]{:S(2)}) copy-start(f32[768,384]{1,0:T(8,128)} %a_ref.1) | copy-start | bytes 3538948
  1.3 1.4 %copy-start.1 = (f32[768,512]{1,0:T(8,128)S(1)}, f32[768,512]{1,0:T(8,128)}, u32[]{:S(2)}) copy-start(f32[768,512]{1,0:T(8,128)} %v_ref.1) | copy-start | bytes 4718596
  2.7 1.0 %copy-start.2 = (f32[2,256,256]{2,1,0:T(8,128)S(1)}, f32[2,256,256]{2,1,0:T(8,128)}, u32[]{:S(2)}) copy-start(f32[2,256,256]{2,1,0:T(8,128)} %t_ref.1) | copy-start | bytes 1572868

commit v2 on v1

v2 whole, which is shorter than its diff:
```python
import jax
import jax.numpy as jnp
from jax import lax
from jax.experimental import pallas as pl
from jax.experimental.pallas import tpu as pltpu
from jax.sharding import PartitionSpec as P

F32 = jnp.float32
BF16 = jnp.bfloat16
RING = 8
NN = (((1,), (0,)), ((), ()))
TN = (((0,), (0,)), ((), ()))
NT = (((1,), (1,)), ((), ()))


def split(x):
    high = x.astype(BF16)
    return high, (x - high.astype(F32)).astype(BF16)


def dot3(left, right, dims):
    (lh, ll), (rh, rl) = left, right
    def one(p, q):
        return lax.dot_general(p, q, dims, preferred_element_type=F32)
    return one(lh, rh) + (one(lh, rl) + one(ll, rh))


def mm(left, right, dims):
    return dot3(split(left), split(right), dims)


def slot_of(q):
    y, xl = q // 2, q % 2
    return xl * 8 + y // 2 % 2 * 4 + y // 4 * 2 + y % 2


SLOT = [slot_of(q) for q in range(16)]
FIRST = sorted(SLOT[:8])


def kernel(a_hbm, v_hbm, t_hbm, upd_ref, a_ref, v_ref, t_ref, ah, al, vh, vl, pt, rs_recv, zx_recv, zcol, vcol,
           zrow, s21, gloc, ga_recv, gtiles, gc_recv, gfull, qh, ql, uh, ul, yt1_ref, load_sems, send_sems, recv_sems):
    width = v_ref.shape[1]
    cols = a_ref.shape[1]
    nb = width // 2
    sub = width // 16
    vsub = cols // 16
    half = sub // 2
    r = lax.axis_index("prow")
    c = lax.axis_index("pcol")
    y, xl = r // 2, r % 2
    chip, k = c // 2, c % 2
    xh, z = chip // 8, chip % 8
    y2, y1, y0 = y // 4, y // 2 % 2, y % 2
    z2, z1, z0 = z // 4, z // 2 % 2, z % 2

    y_peers = [((y + o) % RING * 2 + xl, c) for o in range(1, RING)]
    y_up, y_down = y_peers[0], y_peers[-1]
    z_up = (r, (xh * 8 + (z + 1) % RING) * 2 + k)
    z_down = (r, (xh * 8 + (z + RING - 1) % RING) * 2 + k)
    x_near = (y * 2 + 1 - xl, c)
    x_far = (r, ((1 - xh) * 8 + z) * 2 + k)
    other = (r, chip * 2 + 1 - k)
    x_other = (y * 2 + 1 - xl, chip * 2 + 1 - k)
    v_from = (chip, (xl * 8 + (y2 + z0) % 2 * 4 + (y1 + z1) % 2 * 2 + y0) * 2 + k)
    v_piece = (z2 + xl) % 2 * 4 + (z1 + y0) % 2 * 2 + z0
    v_to = (v_piece * 2 + xh, r * 2 + k)
    v_apart = jnp.logical_or(v_to[0] != r, v_to[1] != c)
    q = (z1 * 4 + z2 * 2 + z0) * 2 + xh
    z_to = (chip, (xl * 8 + y1 * 4 + y2 * 2 + y0) * 2 + k)
    z_from = (q, r * 2 + k)
    z_apart = jnp.logical_or(z_to[0] != r, z_to[1] != c)

    count = [0]
    started = []

    def copy(src, dst, device):
        slot = count[0]
        count[0] += 1
        return pltpu.make_async_remote_copy(
            src_ref=src, dst_ref=dst, send_sem=send_sems.at[slot], recv_sem=recv_sems.at[slot],
            device_id=device, device_id_type=pl.DeviceIdType.MESH)

    def go(op):
        op.start()
        started.append(op)
        return op

    barrier = pltpu.get_barrier_semaphore()

    def greet(device):
        pl.semaphore_signal(barrier, inc=1, device_id=device, device_id_type=pl.DeviceIdType.MESH)

    fixed = [*y_peers, x_near, x_other, z_up, z_down, x_far, other]
    for device in fixed:
        greet(device)

    @pl.when(v_apart)
    def _():
        greet(v_from)

    @pl.when(z_apart)
    def _():
        greet(z_from)

    loads = [pltpu.make_async_copy(src, dst, load_sems.at[i])
             for i, (src, dst) in enumerate(((v_hbm, v_ref), (a_hbm, a_ref), (t_hbm, t_ref)))]
    for load in loads:
        load.start()
    loads[0].wait()
    vh[...], vl[...] = split(v_ref[...])
    loads[1].wait()
    ah[...], al[...] = split(a_ref[...])

    def product(group):
        lanes = pl.ds(pl.multiple_of((group + 4) % 4 * 128, 128), 128)
        pt[lanes, :] = dot3((vh[:, lanes], vl[:, lanes]), (ah[...], al[...]), TN)

    far_group, side = (y + 4) // 2, 1 - 2 * ((y + 1) % 2)
    product(far_group)
    product(far_group + side)

    pl.semaphore_wait(barrier, len(fixed) + v_apart.astype(jnp.int32) + z_apart.astype(jnp.int32))

    def pt_at(part, index):
        return pl.ds(pl.multiple_of((index + RING) % RING * (2 * sub) + part * sub, sub), sub)

    NAMES = ("RA", "LB", "RB", "LA")
    first = {"RA": 0, "LB": 0, "RB": 1, "LA": 1}
    base = {"RA": 0, "LB": 4, "RB": 7, "LA": 10}
    rs = {}

    def rs_at(name, s):
        return pt_at(0 if name[1] == "A" else 1, y + 4 - s if name[0] == "R" else y - 4 + s)

    def rs_send(name, s):
        rs[name, s] = go(copy(pt.at[rs_at(name, s), :], rs_recv.at[base[name] + s], y_up if name[0] == "R" else y_down))

    def rs_round(s):
        for name in NAMES:
            if s - 1 >= first[name]:
                rs[name, s - 1].wait_recv()
                at = rs_at(name, s)
                pt[at, :] = pt[at, :] + rs_recv[base[name] + s - 1]
                rs_send(name, s)

    for name in NAMES:
        rs_send(name, first[name])

    v_rows = pl.ds(pl.multiple_of(v_piece * 2 * vsub, 8), 2 * vsub)
    v_src = pl.ds(pl.multiple_of(k * cols + v_piece * 2 * vsub, 8), 2 * vsub)
    v_copy = copy(v_ref.at[v_src, :], vcol.at[v_rows, :], v_to)

    @pl.when(v_apart)
    def _():
        v_copy.start()

    @pl.when(jnp.logical_not(v_apart))
    def _():
        vcol[v_rows, :] = v_ref[v_src, :]

    product(far_group - side)
    rs_round(1)
    product(far_group + 2)
    rs_round(2)

    half_rows = pl.ds(pl.multiple_of(k * cols, 128), cols)
    s21[...] = dot3((vh[half_rows, nb:], vl[half_rows, nb:]), (vh[half_rows, :nb], vl[half_rows, :nb]), TN)
    rs_round(3)

    def ring(ref_of, me, up, down):
        ops = {}
        last = {"RA": 3, "LB": 3, "RB": 2, "LA": 2}

        def step(s, arrived=None):
            for name in NAMES:
                part = 0 if name[1] == "A" else 1
                index = (me - s + RING) % RING if name[0] == "R" else (me + s) % RING
                if s >= 1 and s - 1 <= last[name]:
                    ops[name, s - 1].wait_recv()
                if s <= last[name]:
                    ref = ref_of(part, index)
                    ops[name, s] = go(copy(ref, ref, up if name[0] == "R" else down))
                if arrived is not None and s >= 1 and s - 1 <= last[name]:
                    arrived(part, index)
        return step

    def zrow_at(core, h, i):
        return zrow.at[core, pl.ds(pl.multiple_of((h * 8 + i) * sub, sub), sub), :]

    v_ring = ring(lambda h, i: vcol.at[pl.ds(pl.multiple_of(i * 2 * vsub + h * vsub, 8), vsub), :], y, y_up, y_down)
    z_ring = ring(lambda h, i: zcol.at[pt_at(h, i), :], y, y_up, y_down)
    row_ring = ring(lambda h, i: zrow_at(k, h, i), z, z_up, z_down)
    g_ring = ring(lambda h, i: gfull.at[(h * 8 + i) * 2 + k], z, z_up, z_down)
    rows_over, g_over = [], []

    def pass_row(h, i):
        rows_over.append(go(copy(zrow_at(k, h, i), zrow_at(k, h, i), other)))

    def pass_g(h, i):
        ref = gfull.at[(h * 8 + i) * 2 + k]
        g_over.append(go(copy(ref, ref, other)))

    @pl.when(v_apart)
    def _():
        v_copy.wait_recv()

    v_ring(0)
    for part, names in ((0, ("RA", "LA")), (1, ("LB", "RB"))):
        at = pt_at(part, y)
        total = pt[at, :]
        for name in names:
            rs[name, 3].wait_recv()
            total = total + rs_recv[base[name] + 3]
        pt[at, :] = total

    def zx_at(part):
        return pl.ds(pl.multiple_of(part * sub, sub), sub)

    x_ops = [go(copy(pt.at[pt_at(part, y), :], zx_recv.at[zx_at(part), :], x_near)) for part in (1 - xl, xl)]
    v_ring(1)

    own, rest = pt_at(xl, y), pt_at(1 - xl, y)
    x_ops[0].wait_recv()
    zcol[own, :] = pt[own, :] + zx_recv[zx_at(xl), :]
    z_rows = pl.ds(pl.multiple_of((z_to[1] // 2) * sub, sub), sub)
    z_copy = copy(zcol.at[own, :], zrow.at[k, z_rows, :], z_to)

    @pl.when(z_apart)
    def _():
        z_copy.start()

    @pl.when(jnp.logical_not(z_apart))
    def _():
        zrow[k, z_rows, :] = zcol[own, :]

    x_ops[1].wait_recv()
    zcol[rest, :] = pt[rest, :] + zx_recv[zx_at(1 - xl), :]
    z_ring(0)
    v_ring(2)

    @pl.when(z_apart)
    def _():
        z_copy.wait_recv()

    mine = zrow_at(k, xh, z)
    part = dot3(split(zrow[k, pl.ds(pl.multiple_of(chip * sub, sub), sub), :]), (vh[half_rows, :], vl[half_rows, :]), NN)
    s_rows = s21[pl.ds(pl.multiple_of(q % 8 * sub, sub), sub), :]
    gloc[:, :nb] = jnp.where(q >= 8, s_rows, part[:, :nb])
    gloc[:, nb:] = part[:, nb:]
    my_half = pl.ds(pl.multiple_of(k * half, half), half)
    its_half = pl.ds(pl.multiple_of((1 - k) * half, half), half)
    ga = [go(copy(gloc.at[its_half, :], ga_recv.at[0], x_other)),
          go(copy(gloc.at[my_half, :], ga_recv.at[1], x_near)),
          go(copy(gloc.at[its_half, :], ga_recv.at[2], other))]
    far_op = go(copy(mine, mine, x_far))
    pass_row(xh, z)
    z_ring(1)
    total = gloc[my_half, :]
    for i in (2, 1, 0):
        ga[i].wait_recv()
        total = total + ga_recv[i]
    for j in range(8):
        gtiles[j] = total[j // 4 * 8:j // 4 * 8 + 8, j % 4 * 128:(j % 4 + 1) * 128]
    gc = [go(copy(gtiles.at[(y + o) % RING], gc_recv.at[o], y_peers[o - 1])) for o in range(1, RING)]
    far_op.wait_recv()
    row_ring(0)
    pass_row(1 - xh, z)
    v_ring(3)
    tile = gtiles[y]
    for o in range(1, RING):
        gc[o - 1].wait_recv()
        tile = tile + gc_recv[o]
    gfull[c, y] = tile
    gd = [go(copy(gfull.at[c, y], gfull.at[c, y], y_peers[o - 1])) for o in range(1, RING)]
    z_ring(2)
    v_ring(4)

    loads[2].wait()
    t1, t2 = split(t_ref[0]), split(t_ref[1])
    v1, v2 = split(vcol[:, :nb]), split(vcol[:, nb:])
    for p, (t, v) in enumerate(((t1, v1), (t2, v2))):
        u_high, u_low = split(dot3(t, v, NT))
        for i in range(8):
            at = SLOT[p * 8 + i] * sub
            uh[at:at + sub, :] = u_high[i * sub:(i + 1) * sub, :]
            ul[at:at + sub, :] = u_low[i * sub:(i + 1) * sub, :]
    for op in gd:
        op.wait_recv()
    ge = go(copy(gfull.at[c], gfull.at[c], x_far))
    pass_g(xh, z)
    row_ring(1, pass_row)
    z_ring(3)
    ge.wait_recv()
    g_ring(0)
    pass_g(1 - xh, z)
    row_ring(2, pass_row)
    z_ring(4)
    yt1 = dot3(t1, split(zcol[:nb, :]), TN)
    yt1_ref[...] = yt1
    qh[:nb, :], ql[:nb, :] = split(yt1)
    qh[nb:, :], ql[nb:, :] = split(dot3(t2, split(zcol[nb:, :]), TN))
    g_ring(1, pass_g)
    row_ring(3, pass_row)
    row_ring(4, pass_row)
    g_ring(2, pass_g)
    for op in rows_over:
        op.wait_recv()

    def tiles(i):
        for h in range(2):
            at = pl.ds(pl.multiple_of(h * cols + i * 128, 128), 128)
            yield h, at, pl.ds(pl.multiple_of(i * 128, 128), 128)

    def early(i, _):
        for h, at, lanes in tiles(i):
            acc = dot3((vh[at, :], vl[at, :]), (qh[...], ql[...]), NN)
            upd_ref[at, :] = -acc - dot3(split(zrow[h, :, lanes]), (uh[...], ul[...]), TN)
        return 0

    def late(i, _):
        for h, at, lanes in tiles(i):
            acc = dot3((vh[at, :], vl[at, :]), (qh[...], ql[...]), NN)
            kept = jnp.concatenate([zrow[h, s * sub:(s + 1) * sub, lanes] for s in FIRST], axis=0)
            upd_ref[at, :] = upd_ref[at, :] - acc - dot3(split(kept), (uh[:nb, :], ul[:nb, :]), TN)
        return 0

    lax.fori_loop(0, 2, early, 0)
    g_ring(3, pass_g)
    lax.fori_loop(2, 3, early, 0)
    g_ring(4, pass_g)
    for op in g_over:
        op.wait_recv()

    def block(row, col):
        lanes = []
        for j in (2 * col, 2 * col + 1):
            found = [gfull[SLOT[i] * 2 + core, h * 4 + j]
                     for i in range(row * 8, row * 8 + 8) for core in range(2) for h in range(2)]
            lanes.append(jnp.concatenate(found, axis=0))
        return jnp.concatenate(lanes, axis=1)

    g11, g12, s_21, g22 = block(0, 0), block(0, 1), block(1, 0), block(1, 1)
    s_21s = split(s_21)
    s_12s = split(s_21.T)
    e = dot3(s_12s, t2, NN)
    es = split(e)
    m1 = dot3(t1, split(dot3(split(g11), t1, NN)), TN)
    m1s = split(m1)
    kk = dot3(t1, split(g12), TN) - 0.5 * dot3(m1s, s_12s, TN)
    kks = split(kk)
    jj = dot3(s_21s, kks, NN)
    m2 = dot3(t2, split(dot3(split(g22 - jj - jj.T), t2, NN)), TN)
    h12s = split(0.5 * dot3(m1s, es, NN) - dot3(kks, t2, NN))
    qh[:nb, :], ql[:nb, :] = split(dot3(h12s, v2, NT) - dot3(m1s, v1, NT))
    low_q = dot3(h12s, v1, (((0,), (1,)), ((), ()))) - dot3(split(m2), v2, NT)
    qh[nb:, :], ql[nb:, :] = split(low_q - dot3(es, split(yt1_ref[...]), TN))
    u_high, u_low = split(-dot3(t1, split(dot3(es, v2, NT)), NN))
    for at, s in enumerate(FIRST):
        i = SLOT.index(s)
        uh[at * sub:(at + 1) * sub, :] = u_high[i * sub:(i + 1) * sub, :]
        ul[at * sub:(at + 1) * sub, :] = u_low[i * sub:(i + 1) * sub, :]
    lax.fori_loop(0, cols // 128, late, 0)

    for op in started:
        op.wait_send()

    @pl.when(v_apart)
    def _():
        v_copy.wait_send()

    @pl.when(z_apart)
    def _():
        z_copy.wait_send()


COPIES = 14 + 2 + 2 + 14 + 14 + (1 + 14 + 16) + (3 + 7 + 7 + 1 + 14 + 16)


def body(matrix, reflectors, factors):
    rows, cols = matrix.shape
    width = reflectors.shape[1]
    nb = width // 2
    sub = width // 16
    vmem = pl.BlockSpec(memory_space=pltpu.VMEM)
    update = pl.pallas_call(
        kernel,
        out_shape=jax.ShapeDtypeStruct((rows, cols), F32),
        in_specs=[pl.BlockSpec(memory_space=pltpu.HBM)] * 3,
        out_specs=vmem,
        scratch_shapes=[
            pltpu.VMEM((rows, cols), F32),
            pltpu.VMEM((rows, width), F32),
            pltpu.VMEM(factors.shape, F32),
            pltpu.VMEM((rows, cols), BF16),
            pltpu.VMEM((rows, cols), BF16),
            pltpu.VMEM((rows, width), BF16),
            pltpu.VMEM((rows, width), BF16),
            pltpu.VMEM((width, cols), F32),
            pltpu.VMEM((14, sub, cols), F32),
            pltpu.VMEM((2 * sub, cols), F32),
            pltpu.VMEM((width, cols), F32),
            pltpu.VMEM((cols, width), F32),
            pltpu.VMEM((2, width, cols), F32),
            pltpu.VMEM((nb, nb), F32),
            pltpu.VMEM((sub, width), F32),
            pltpu.VMEM((3, sub // 2, width), F32),
            pltpu.VMEM((8, 8, 128), F32),
            pltpu.VMEM((8, 8, 128), F32),
            pltpu.VMEM((32, 8, 8, 128), F32),
            pltpu.VMEM((width, cols), BF16),
            pltpu.VMEM((width, cols), BF16),
            pltpu.VMEM((width, cols), BF16),
            pltpu.VMEM((width, cols), BF16),
            pltpu.VMEM((nb, cols), F32),
            pltpu.SemaphoreType.DMA((3,)),
            pltpu.SemaphoreType.DMA((COPIES,)),
            pltpu.SemaphoreType.DMA((COPIES,)),
        ],
        compiler_params=pltpu.CompilerParams(
            collective_id=0, has_side_effects=True, vmem_limit_bytes=60 * 1024 * 1024),
        name="two_panels",
    )(matrix, reflectors, factors)
    return matrix + update


def solution(mesh):
    return jax.shard_map(
        body,
        mesh=mesh,
        in_specs=(P("prow", "pcol"), P("prow", None), P()),
        out_specs=P("prow", "pcol"),
        check_vma=False,
    )
```

time: 102 us -> 92 us (0.902)
  Pallas kernels: 97.4 us -> 89.4 us
  local copies, waits for them, and re-layouts: 3.72 us -> 0.01 us
  other arithmetic: 1.13 us -> 2.4 us
    pallas_call x1, Pallas kernels: 97.4 us -> 89.4 us  [body(): pl.pallas_call(kernel, out_shape=jax.ShapeDtypeStruct((rows, cols), F32),...]
    unnamed x6 -> x2, local copies, waits for them, and re-layouts: 3.72 us -> 0.01 us
    add x1, other arithmetic: 1.13 us -> 2.4 us  [body(): return matrix + update]
where the time goes in v2:
time: 92 us; the launch traced here: 91.8 us
  Pallas kernels  89.4 us (97%)
  other arithmetic  2.4 us (3%)
    pallas_call x1, Pallas kernels, body(): pl.pallas_call(kernel, out_shape=jax.ShapeDtypeStruct((rows, cols), F32),...  89.4 us
    add x1, other arithmetic, body(): return matrix + update  2.4 us

profile of v2, /device:TPU:1, one launch (start us, length us, event | category | flops | bytes accessed | tf_op | source)
XLA Modules:
  0.0 91.8 jit_solution(15040452235479645329)
XLA Ops:
  0.0 0.0 copy-start
  0.0 89.4 %two_panels.1 = f32[768,384]{1,0:T(8,128)} custom-call(f32[768,384]{1,0:T(8,128)} %a_hbm.1, f32[768,512]{1,0:T(8,128)} %v_hbm.1, f32[2,256,256]{2,1,0:T(8,128)} %t_hbm.1), custom_call_target="tpu_custom_call" | custom-call | tf_op jit(solution)/shard_map/two_panels/pallas_call | solution.py:386
  89.4 0.0 copy-done
  89.4 2.4 %add.3 = f32[768,384]{1,0:T(8,128)} add(f32[768,384]{1,0:T(8,128)S(1)} %copy-done, f32[768,384]{1,0:T(8,128)} %two_panels.1) | non-fusion elementwise | flops 294912 | bytes 3538944 | tf_op jit(solution)/shard_map/add | solution.py:424
Async XLA Ops:
  0.0 89.4 %copy-start = (f32[768,384]{1,0:T(8,128)S(1)}, f32[768,384]{1,0:T(8,128)}, u32[]{:S(2)}) copy-start(f32[768,384]{1,0:T(8,128)} %a_hbm.1) | copy-start | bytes 3538948

commit v3 on v2

--- a/solution.py
+++ b/solution.py
@@ -31,7 +31,7 @@
 
 def slot_of(q):
     y, xl = q // 2, q % 2
-    return xl * 8 + y // 2 % 2 * 4 + y // 4 * 2 + y % 2
+    return (y // 2 % 2 * 4 + y // 4 * 2 + y % 2) * 2 + xl
 
 
 SLOT = [slot_of(q) for q in range(16)]
@@ -56,8 +56,9 @@
 
     y_peers = [((y + o) % RING * 2 + xl, c) for o in range(1, RING)]
     y_up, y_down = y_peers[0], y_peers[-1]
-    z_up = (r, (xh * 8 + (z + 1) % RING) * 2 + k)
-    z_down = (r, (xh * 8 + (z + RING - 1) % RING) * 2 + k)
+    mine = z * 2 + xh
+    y_at = {1: y_peers[0], 2: y_peers[1], -2: y_peers[-2], -1: y_peers[-1]}
+    z_at = {o: (r, (xh * 8 + (z + o + RING) % RING) * 2 + k) for o in (1, 2, -2, -1)}
     x_near = (y * 2 + 1 - xl, c)
     x_far = (r, ((1 - xh) * 8 + z) * 2 + k)
     other = (r, chip * 2 + 1 - k)
@@ -91,7 +92,7 @@
     def greet(device):
         pl.semaphore_signal(barrier, inc=1, device_id=device, device_id_type=pl.DeviceIdType.MESH)
 
-    fixed = [*y_peers, x_near, x_other, z_up, z_down, x_far, other]
+    fixed = [*y_peers, x_near, x_other, *z_at.values(), x_far, other]
     for device in fixed:
         greet(device)
 
@@ -168,44 +169,61 @@
     s21[...] = dot3((vh[half_rows, nb:], vl[half_rows, nb:]), (vh[half_rows, :nb], vl[half_rows, :nb]), TN)
     rs_round(3)
 
-    def ring(ref_of, me, up, down):
+    def gather(whole, halves, me, at):
         ops = {}
-        last = {"RA": 3, "LB": 3, "RB": 2, "LA": 2}
-
-        def step(s, arrived=None):
-            for name in NAMES:
-                part = 0 if name[1] == "A" else 1
-                index = (me - s + RING) % RING if name[0] == "R" else (me + s) % RING
-                if s >= 1 and s - 1 <= last[name]:
-                    ops[name, s - 1].wait_recv()
-                if s <= last[name]:
-                    ref = ref_of(part, index)
-                    ops[name, s] = go(copy(ref, ref, up if name[0] == "R" else down))
-                if arrived is not None and s >= 1 and s - 1 <= last[name]:
-                    arrived(part, index)
-        return step
-
-    def zrow_at(core, h, i):
-        return zrow.at[core, pl.ds(pl.multiple_of((h * 8 + i) * sub, sub), sub), :]
-
-    v_ring = ring(lambda h, i: vcol.at[pl.ds(pl.multiple_of(i * 2 * vsub + h * vsub, 8), vsub), :], y, y_up, y_down)
-    z_ring = ring(lambda h, i: zcol.at[pt_at(h, i), :], y, y_up, y_down)
-    row_ring = ring(lambda h, i: zrow_at(k, h, i), z, z_up, z_down)
-    g_ring = ring(lambda h, i: gfull.at[(h * 8 + i) * 2 + k], z, z_up, z_down)
-    rows_over, g_over = [], []
-
-    def pass_row(h, i):
-        rows_over.append(go(copy(zrow_at(k, h, i), zrow_at(k, h, i), other)))
-
-    def pass_g(h, i):
-        ref = gfull.at[(h * 8 + i) * 2 + k]
-        g_over.append(go(copy(ref, ref, other)))
+
+        def near():
+            for o in (1, -1, 2, -2):
+                ops[o] = go(copy(whole(me), whole(me), at[o]))
+
+        def on():
+            for o in (2, -2):
+                ops[o].wait_recv()
+                index = (me - o + RING) % RING
+                half_ref = halves(0 if o > 0 else 1, index)
+                ops[o, 1] = go(copy(whole(index), whole(index), at[o // 2]))
+                ops[o, 2] = go(copy(half_ref, half_ref, at[o]))
+
+        def last():
+            for o in (2, -2):
+                ops[o // 2].wait_recv()
+                ops[o, 1].wait_recv()
+                ops[o, 2].wait_recv()
+
+        return near, on, last
+
+    def slots(index):
+        return pl.ds(pl.multiple_of(index * 2 * sub, sub), 2 * sub)
+
+    def row_chunk(index):
+        return zrow.at[k, slots(index), :]
+
+    def row_half(part, index):
+        return zrow.at[k, pl.ds(pl.multiple_of(index * 2 * sub + part * sub, sub), sub), :]
+
+    def g_chunk(index):
+        return gfull.at[k, pl.ds(index * 2, 2)]
+
+    def v_rows_of(start, size):
+        return vcol.at[pl.ds(pl.multiple_of(start, 8), size), :]
+
+    v_gather = gather(lambda i: v_rows_of(i * 2 * vsub, 2 * vsub),
+                      lambda h, i: v_rows_of(i * 2 * vsub + h * vsub, vsub), y, y_at)
+    z_gather = gather(lambda i: zcol.at[slots(i), :], lambda h, i: zcol.at[pt_at(h, i), :], y, y_at)
+    row_gather = gather(row_chunk, row_half, z, z_at)
+    g_gather = gather(g_chunk, lambda h, i: gfull.at[k, pl.ds(i * 2 + h, 1)], z, z_at)
+    over = {row_chunk: [], g_chunk: []}
+
+    def pass_on(chunk, offsets):
+        for o in offsets:
+            ref = chunk((z + o + RING) % RING)
+            over[chunk].append(go(copy(ref, ref, other)))
 
     @pl.when(v_apart)
     def _():
         v_copy.wait_recv()
 
-    v_ring(0)
+    v_gather[0]()
     for part, names in ((0, ("RA", "LA")), (1, ("LB", "RB"))):
         at = pt_at(part, y)
         total = pt[at, :]
@@ -218,12 +236,12 @@
         return pl.ds(pl.multiple_of(part * sub, sub), sub)
 
     x_ops = [go(copy(pt.at[pt_at(part, y), :], zx_recv.at[zx_at(part), :], x_near)) for part in (1 - xl, xl)]
-    v_ring(1)
+    v_gather[1]()
 
     own, rest = pt_at(xl, y), pt_at(1 - xl, y)
     x_ops[0].wait_recv()
     zcol[own, :] = pt[own, :] + zx_recv[zx_at(xl), :]
-    z_rows = pl.ds(pl.multiple_of((z_to[1] // 2) * sub, sub), sub)
+    z_rows = pl.ds(pl.multiple_of(((y1 * 4 + y2 * 2 + y0) * 2 + xl) * sub, sub), sub)
     z_copy = copy(zcol.at[own, :], zrow.at[k, z_rows, :], z_to)
 
     @pl.when(z_apart)
@@ -236,15 +254,14 @@
 
     x_ops[1].wait_recv()
     zcol[rest, :] = pt[rest, :] + zx_recv[zx_at(1 - xl), :]
-    z_ring(0)
-    v_ring(2)
+    z_gather[0]()
 
     @pl.when(z_apart)
     def _():
         z_copy.wait_recv()
 
-    mine = zrow_at(k, xh, z)
-    part = dot3(split(zrow[k, pl.ds(pl.multiple_of(chip * sub, sub), sub), :]), (vh[half_rows, :], vl[half_rows, :]), NN)
+    own_slot = pl.ds(pl.multiple_of(mine * sub, sub), sub)
+    part = dot3(split(zrow[k, own_slot, :]), (vh[half_rows, :], vl[half_rows, :]), NN)
     s_rows = s21[pl.ds(pl.multiple_of(q % 8 * sub, sub), sub), :]
     gloc[:, :nb] = jnp.where(q >= 8, s_rows, part[:, :nb])
     gloc[:, nb:] = part[:, nb:]
@@ -253,9 +270,8 @@
     ga = [go(copy(gloc.at[its_half, :], ga_recv.at[0], x_other)),
           go(copy(gloc.at[my_half, :], ga_recv.at[1], x_near)),
           go(copy(gloc.at[its_half, :], ga_recv.at[2], other))]
-    far_op = go(copy(mine, mine, x_far))
-    pass_row(xh, z)
-    z_ring(1)
+    far_op = go(copy(zrow.at[k, own_slot, :], zrow.at[k, own_slot, :], x_far))
+    z_gather[1]()
     total = gloc[my_half, :]
     for i in (2, 1, 0):
         ga[i].wait_recv()
@@ -264,17 +280,17 @@
         gtiles[j] = total[j // 4 * 8:j // 4 * 8 + 8, j % 4 * 128:(j % 4 + 1) * 128]
     gc = [go(copy(gtiles.at[(y + o) % RING], gc_recv.at[o], y_peers[o - 1])) for o in range(1, RING)]
     far_op.wait_recv()
-    row_ring(0)
-    pass_row(1 - xh, z)
-    v_ring(3)
+    row_gather[0]()
+    pass_on(row_chunk, (0,))
     tile = gtiles[y]
     for o in range(1, RING):
         gc[o - 1].wait_recv()
         tile = tile + gc_recv[o]
-    gfull[c, y] = tile
-    gd = [go(copy(gfull.at[c, y], gfull.at[c, y], y_peers[o - 1])) for o in range(1, RING)]
-    z_ring(2)
-    v_ring(4)
+    gfull[k, mine, y] = tile
+    gd = [go(copy(gfull.at[k, mine, y], gfull.at[k, mine, y], y_peers[o - 1])) for o in range(1, RING)]
+    row_gather[1]()
+    pass_on(row_chunk, (2, -2))
+    v_gather[2]()
 
     loads[2].wait()
     t1, t2 = split(t_ref[0]), split(t_ref[1])
@@ -287,24 +303,18 @@
             ul[at:at + sub, :] = u_low[i * sub:(i + 1) * sub, :]
     for op in gd:
         op.wait_recv()
-    ge = go(copy(gfull.at[c], gfull.at[c], x_far))
-    pass_g(xh, z)
-    row_ring(1, pass_row)
-    z_ring(3)
+    ge = go(copy(gfull.at[k, mine], gfull.at[k, mine], x_far))
+    row_gather[2]()
+    pass_on(row_chunk, (1, -1, 3, -3, 4))
+    z_gather[2]()
     ge.wait_recv()
-    g_ring(0)
-    pass_g(1 - xh, z)
-    row_ring(2, pass_row)
-    z_ring(4)
+    g_gather[0]()
+    pass_on(g_chunk, (0,))
     yt1 = dot3(t1, split(zcol[:nb, :]), TN)
     yt1_ref[...] = yt1
     qh[:nb, :], ql[:nb, :] = split(yt1)
     qh[nb:, :], ql[nb:, :] = split(dot3(t2, split(zcol[nb:, :]), TN))
-    g_ring(1, pass_g)
-    row_ring(3, pass_row)
-    row_ring(4, pass_row)
-    g_ring(2, pass_g)
-    for op in rows_over:
+    for op in over[row_chunk]:
         op.wait_recv()
 
     def tiles(i):
@@ -325,17 +335,19 @@
             upd_ref[at, :] = upd_ref[at, :] - acc - dot3(split(kept), (uh[:nb, :], ul[:nb, :]), TN)
         return 0
 
-    lax.fori_loop(0, 2, early, 0)
-    g_ring(3, pass_g)
-    lax.fori_loop(2, 3, early, 0)
-    g_ring(4, pass_g)
-    for op in g_over:
+    lax.fori_loop(0, 1, early, 0)
+    g_gather[1]()
+    pass_on(g_chunk, (2, -2))
+    lax.fori_loop(1, 3, early, 0)
+    g_gather[2]()
+    pass_on(g_chunk, (1, -1, 3, -3, 4))
+    for op in over[g_chunk]:
         op.wait_recv()
 
     def block(row, col):
         lanes = []
         for j in (2 * col, 2 * col + 1):
-            found = [gfull[SLOT[i] * 2 + core, h * 4 + j]
+            found = [gfull[core, SLOT[i], h * 4 + j]
                      for i in range(row * 8, row * 8 + 8) for core in range(2) for h in range(2)]
             lanes.append(jnp.concatenate(found, axis=0))
         return jnp.concatenate(lanes, axis=1)
@@ -374,7 +386,7 @@
         z_copy.wait_send()
 
 
-COPIES = 14 + 2 + 2 + 14 + 14 + (1 + 14 + 16) + (3 + 7 + 7 + 1 + 14 + 16)
+COPIES = 14 + 2 + 2 + 8 + 8 + (1 + 8 + 8) + (3 + 7 + 7 + 1 + 8 + 8)
 
 
 def body(matrix, reflectors, factors):
@@ -407,7 +419,7 @@
             pltpu.VMEM((3, sub // 2, width), F32),
             pltpu.VMEM((8, 8, 128), F32),
             pltpu.VMEM((8, 8, 128), F32),
-            pltpu.VMEM((32, 8, 8, 128), F32),
+            pltpu.VMEM((2, 16, 8, 8, 128), F32),
             pltpu.VMEM((width, cols), BF16),
             pltpu.VMEM((width, cols), BF16),
             pltpu.VMEM((width, cols), BF16),

time: 92 us -> 96.5 us (1.049)
  the two profiles are of different devices: /device:TPU:1 before, /device:TPU:7 now
where the time goes in v3:
time: 96.5 us; the launch traced here: 96.4 us
  Pallas kernels  93.9 us (97%)
  other arithmetic  2.4 us (2%)
    pallas_call x1, Pallas kernels, body(): pl.pallas_call(kernel, out_shape=jax.ShapeDtypeStruct((rows, cols), F32),...  93.9 us
    add x1, other arithmetic, body(): return matrix + update  2.4 us

profile of v3, /device:TPU:7, one launch (start us, length us, event | category | flops | bytes accessed | tf_op | source)
XLA Modules:
  0.0 96.4 jit_solution(11444321208549709806)
XLA Ops:
  0.0 0.0 copy-start
  0.0 93.9 %two_panels.1 = f32[768,384]{1,0:T(8,128)} custom-call(f32[768,384]{1,0:T(8,128)} %a_hbm.1, f32[768,512]{1,0:T(8,128)} %v_hbm.1, f32[2,256,256]{2,1,0:T(8,128)} %t_hbm.1), custom_call_target="tpu_custom_call" | custom-call | tf_op jit(solution)/shard_map/two_panels/pallas_call | solution.py:398
  94.0 0.0 copy-done
  94.0 2.4 %add.3 = f32[768,384]{1,0:T(8,128)} add(f32[768,384]{1,0:T(8,128)S(1)} %copy-done, f32[768,384]{1,0:T(8,128)} %two_panels.1) | non-fusion elementwise | flops 294912 | bytes 3538944 | tf_op jit(solution)/shard_map/add | solution.py:436
Async XLA Ops:
  0.0 94.0 %copy-start = (f32[768,384]{1,0:T(8,128)S(1)}, f32[768,384]{1,0:T(8,128)}, u32[]{:S(2)}) copy-start(f32[768,384]{1,0:T(8,128)} %a_hbm.1) | copy-start | bytes 3538948

commit v4 on v3

--- a/solution.py
+++ b/solution.py
@@ -169,6 +169,24 @@
     s21[...] = dot3((vh[half_rows, nb:], vl[half_rows, nb:]), (vh[half_rows, :nb], vl[half_rows, :nb]), TN)
     rs_round(3)
 
+    def ring(half_of, me, up, down):
+        ops = {}
+        last = {"RA": 3, "LB": 3, "RB": 2, "LA": 2}
+
+        def step(s, arrived=None):
+            for name in NAMES:
+                part = 0 if name[1] == "A" else 1
+                index = (me - s + RING) % RING if name[0] == "R" else (me + s) % RING
+                if s >= 1 and s - 1 <= last[name]:
+                    ops[name, s - 1].wait_recv()
+                if s <= last[name]:
+                    ref = half_of(part, index)
+                    ops[name, s] = go(copy(ref, ref, up if name[0] == "R" else down))
+                if arrived is not None and s >= 1 and s - 1 <= last[name]:
+                    arrived(part, index)
+
+        return step
+
     def gather(whole, halves, me, at):
         ops = {}
 
@@ -183,21 +201,16 @@
                 half_ref = halves(0 if o > 0 else 1, index)
                 ops[o, 1] = go(copy(whole(index), whole(index), at[o // 2]))
                 ops[o, 2] = go(copy(half_ref, half_ref, at[o]))
+            for o in (1, -1):
+                ops[o].wait_recv()
 
         def last():
             for o in (2, -2):
-                ops[o // 2].wait_recv()
                 ops[o, 1].wait_recv()
                 ops[o, 2].wait_recv()
 
         return near, on, last
 
-    def slots(index):
-        return pl.ds(pl.multiple_of(index * 2 * sub, sub), 2 * sub)
-
-    def row_chunk(index):
-        return zrow.at[k, slots(index), :]
-
     def row_half(part, index):
         return zrow.at[k, pl.ds(pl.multiple_of(index * 2 * sub + part * sub, sub), sub), :]
 
@@ -207,23 +220,26 @@
     def v_rows_of(start, size):
         return vcol.at[pl.ds(pl.multiple_of(start, 8), size), :]
 
-    v_gather = gather(lambda i: v_rows_of(i * 2 * vsub, 2 * vsub),
-                      lambda h, i: v_rows_of(i * 2 * vsub + h * vsub, vsub), y, y_at)
-    z_gather = gather(lambda i: zcol.at[slots(i), :], lambda h, i: zcol.at[pt_at(h, i), :], y, y_at)
-    row_gather = gather(row_chunk, row_half, z, z_at)
+    v_ring = ring(lambda h, i: v_rows_of(i * 2 * vsub + h * vsub, vsub), y, y_up, y_down)
+    z_ring = ring(lambda h, i: zcol.at[pt_at(h, i), :], y, y_up, y_down)
+    row_ring = ring(row_half, z, z_at[1], z_at[-1])
     g_gather = gather(g_chunk, lambda h, i: gfull.at[k, pl.ds(i * 2 + h, 1)], z, z_at)
-    over = {row_chunk: [], g_chunk: []}
-
-    def pass_on(chunk, offsets):
+    rows_over, g_over = [], []
+
+    def pass_row(part, index):
+        ref = row_half(part, index)
+        rows_over.append(go(copy(ref, ref, other)))
+
+    def pass_g(offsets):
         for o in offsets:
-            ref = chunk((z + o + RING) % RING)
-            over[chunk].append(go(copy(ref, ref, other)))
+            ref = g_chunk((z + o + RING) % RING)
+            g_over.append(go(copy(ref, ref, other)))
 
     @pl.when(v_apart)
     def _():
         v_copy.wait_recv()
 
-    v_gather[0]()
+    v_ring(0)
     for part, names in ((0, ("RA", "LA")), (1, ("LB", "RB"))):
         at = pt_at(part, y)
         total = pt[at, :]
@@ -236,7 +252,7 @@
         return pl.ds(pl.multiple_of(part * sub, sub), sub)
 
     x_ops = [go(copy(pt.at[pt_at(part, y), :], zx_recv.at[zx_at(part), :], x_near)) for part in (1 - xl, xl)]
-    v_gather[1]()
+    v_ring(1)
 
     own, rest = pt_at(xl, y), pt_at(1 - xl, y)
     x_ops[0].wait_recv()
@@ -254,13 +270,15 @@
 
     x_ops[1].wait_recv()
     zcol[rest, :] = pt[rest, :] + zx_recv[zx_at(1 - xl), :]
-    z_gather[0]()
+    z_ring(0)
+    v_ring(2)
 
     @pl.when(z_apart)
     def _():
         z_copy.wait_recv()
 
     own_slot = pl.ds(pl.multiple_of(mine * sub, sub), sub)
+    far_op = go(copy(zrow.at[k, own_slot, :], zrow.at[k, own_slot, :], x_far))
     part = dot3(split(zrow[k, own_slot, :]), (vh[half_rows, :], vl[half_rows, :]), NN)
     s_rows = s21[pl.ds(pl.multiple_of(q % 8 * sub, sub), sub), :]
     gloc[:, :nb] = jnp.where(q >= 8, s_rows, part[:, :nb])
@@ -270,8 +288,10 @@
     ga = [go(copy(gloc.at[its_half, :], ga_recv.at[0], x_other)),
           go(copy(gloc.at[my_half, :], ga_recv.at[1], x_near)),
           go(copy(gloc.at[its_half, :], ga_recv.at[2], other))]
-    far_op = go(copy(zrow.at[k, own_slot, :], zrow.at[k, own_slot, :], x_far))
-    z_gather[1]()
+    far_op.wait_recv()
+    row_ring(0)
+    pass_row(xh, z)
+    z_ring(1)
     total = gloc[my_half, :]
     for i in (2, 1, 0):
         ga[i].wait_recv()
@@ -279,18 +299,18 @@
     for j in range(8):
         gtiles[j] = total[j // 4 * 8:j // 4 * 8 + 8, j % 4 * 128:(j % 4 + 1) * 128]
     gc = [go(copy(gtiles.at[(y + o) % RING], gc_recv.at[o], y_peers[o - 1])) for o in range(1, RING)]
-    far_op.wait_recv()
-    row_gather[0]()
-    pass_on(row_chunk, (0,))
+    pass_row(1 - xh, z)
+    row_ring(1, pass_row)
+    v_ring(3)
     tile = gtiles[y]
     for o in range(1, RING):
         gc[o - 1].wait_recv()
         tile = tile + gc_recv[o]
     gfull[k, mine, y] = tile
     gd = [go(copy(gfull.at[k, mine, y], gfull.at[k, mine, y], y_peers[o - 1])) for o in range(1, RING)]
-    row_gather[1]()
-    pass_on(row_chunk, (2, -2))
-    v_gather[2]()
+    row_ring(2, pass_row)
+    z_ring(2)
+    v_ring(4)
 
     loads[2].wait()
     t1, t2 = split(t_ref[0]), split(t_ref[1])
@@ -304,19 +324,17 @@
     for op in gd:
         op.wait_recv()
     ge = go(copy(gfull.at[k, mine], gfull.at[k, mine], x_far))
-    row_gather[2]()
-    pass_on(row_chunk, (1, -1, 3, -3, 4))
-    z_gather[2]()
+    row_ring(3, pass_row)
+    z_ring(3)
     ge.wait_recv()
     g_gather[0]()
-    pass_on(g_chunk, (0,))
+    pass_g((0,))
+    row_ring(4, pass_row)
+    z_ring(4)
     yt1 = dot3(t1, split(zcol[:nb, :]), TN)
     yt1_ref[...] = yt1
     qh[:nb, :], ql[:nb, :] = split(yt1)
     qh[nb:, :], ql[nb:, :] = split(dot3(t2, split(zcol[nb:, :]), TN))
-    for op in over[row_chunk]:
-        op.wait_recv()
-
     def tiles(i):
         for h in range(2):
             at = pl.ds(pl.multiple_of(h * cols + i * 128, 128), 128)
@@ -335,13 +353,14 @@
             upd_ref[at, :] = upd_ref[at, :] - acc - dot3(split(kept), (uh[:nb, :], ul[:nb, :]), TN)
         return 0
 
-    lax.fori_loop(0, 1, early, 0)
     g_gather[1]()
-    pass_on(g_chunk, (2, -2))
-    lax.fori_loop(1, 3, early, 0)
+    pass_g((1, -1, 2, -2))
+    for op in rows_over:
+        op.wait_recv()
+    lax.fori_loop(0, 3, early, 0)
     g_gather[2]()
-    pass_on(g_chunk, (1, -1, 3, -3, 4))
-    for op in over[g_chunk]:
+    pass_g((3, -3, 4))
+    for op in g_over:
         op.wait_recv()
 
     def block(row, col):
@@ -386,7 +405,7 @@
         z_copy.wait_send()
 
 
-COPIES = 14 + 2 + 2 + 8 + 8 + (1 + 8 + 8) + (3 + 7 + 7 + 1 + 8 + 8)
+COPIES = 14 + 2 + 2 + 14 + 14 + (1 + 14 + 16) + (3 + 7 + 7 + 1 + 8 + 8)
 
 
 def body(matrix, reflectors, factors):

time: 96.5 us -> 89.9 us (0.932)
  the two profiles are of different devices: /device:TPU:7 before, /device:TPU:1 now
where the time goes in v4:
time: 89.9 us; the launch traced here: 89.8 us
  Pallas kernels  87.4 us (97%)
  other arithmetic  2.4 us (3%)
    pallas_call x1, Pallas kernels, body(): pl.pallas_call(kernel, out_shape=jax.ShapeDtypeStruct((rows, cols), F32),...  87.4 us
    add x1, other arithmetic, body(): return matrix + update  2.4 us

profile of v4, /device:TPU:1, one launch (start us, length us, event | category | flops | bytes accessed | tf_op | source)
XLA Modules:
  0.0 89.8 jit_solution(14440427575766163608)
XLA Ops:
  0.0 0.0 copy-start
  0.0 87.4 %two_panels.1 = f32[768,384]{1,0:T(8,128)} custom-call(f32[768,384]{1,0:T(8,128)} %a_hbm.1, f32[768,512]{1,0:T(8,128)} %v_hbm.1, f32[2,256,256]{2,1,0:T(8,128)} %t_hbm.1), custom_call_target="tpu_custom_call" | custom-call | tf_op jit(solution)/shard_map/two_panels/pallas_call | solution.py:417
  87.4 0.0 copy-done
  87.4 2.4 %add.3 = f32[768,384]{1,0:T(8,128)} add(f32[768,384]{1,0:T(8,128)S(1)} %copy-done, f32[768,384]{1,0:T(8,128)} %two_panels.1) | non-fusion elementwise | flops 294912 | bytes 3538944 | tf_op jit(solution)/shard_map/add | solution.py:455
Async XLA Ops:
  0.0 87.4 %copy-start = (f32[768,384]{1,0:T(8,128)S(1)}, f32[768,384]{1,0:T(8,128)}, u32[]{:S(2)}) copy-start(f32[768,384]{1,0:T(8,128)} %a_hbm.1) | copy-start | bytes 3538948

commit v5 on v4

--- a/solution.py
+++ b/solution.py
@@ -152,14 +152,6 @@
     v_src = pl.ds(pl.multiple_of(k * cols + v_piece * 2 * vsub, 8), 2 * vsub)
     v_copy = copy(v_ref.at[v_src, :], vcol.at[v_rows, :], v_to)
 
-    @pl.when(v_apart)
-    def _():
-        v_copy.start()
-
-    @pl.when(jnp.logical_not(v_apart))
-    def _():
-        vcol[v_rows, :] = v_ref[v_src, :]
-
     product(far_group - side)
     rs_round(1)
     product(far_group + 2)
@@ -168,6 +160,14 @@
     half_rows = pl.ds(pl.multiple_of(k * cols, 128), cols)
     s21[...] = dot3((vh[half_rows, nb:], vl[half_rows, nb:]), (vh[half_rows, :nb], vl[half_rows, :nb]), TN)
     rs_round(3)
+
+    @pl.when(v_apart)
+    def _():
+        v_copy.start()
+
+    @pl.when(jnp.logical_not(v_apart))
+    def _():
+        vcol[v_rows, :] = v_ref[v_src, :]
 
     def ring(half_of, me, up, down):
         ops = {}
@@ -235,11 +235,6 @@
             ref = g_chunk((z + o + RING) % RING)
             g_over.append(go(copy(ref, ref, other)))
 
-    @pl.when(v_apart)
-    def _():
-        v_copy.wait_recv()
-
-    v_ring(0)
     for part, names in ((0, ("RA", "LA")), (1, ("LB", "RB"))):
         at = pt_at(part, y)
         total = pt[at, :]
@@ -252,7 +247,6 @@
         return pl.ds(pl.multiple_of(part * sub, sub), sub)
 
     x_ops = [go(copy(pt.at[pt_at(part, y), :], zx_recv.at[zx_at(part), :], x_near)) for part in (1 - xl, xl)]
-    v_ring(1)
 
     own, rest = pt_at(xl, y), pt_at(1 - xl, y)
     x_ops[0].wait_recv()
@@ -271,7 +265,12 @@
     x_ops[1].wait_recv()
     zcol[rest, :] = pt[rest, :] + zx_recv[zx_at(1 - xl), :]
     z_ring(0)
-    v_ring(2)
+
+    @pl.when(v_apart)
+    def _():
+        v_copy.wait_recv()
+
+    v_ring(0)
 
     @pl.when(z_apart)
     def _():
@@ -292,6 +291,7 @@
     row_ring(0)
     pass_row(xh, z)
     z_ring(1)
+    v_ring(1)
     total = gloc[my_half, :]
     for i in (2, 1, 0):
         ga[i].wait_recv()
@@ -301,7 +301,7 @@
     gc = [go(copy(gtiles.at[(y + o) % RING], gc_recv.at[o], y_peers[o - 1])) for o in range(1, RING)]
     pass_row(1 - xh, z)
     row_ring(1, pass_row)
-    v_ring(3)
+    v_ring(2)
     tile = gtiles[y]
     for o in range(1, RING):
         gc[o - 1].wait_recv()
@@ -310,17 +310,8 @@
     gd = [go(copy(gfull.at[k, mine, y], gfull.at[k, mine, y], y_peers[o - 1])) for o in range(1, RING)]
     row_ring(2, pass_row)
     z_ring(2)
-    v_ring(4)
-
-    loads[2].wait()
-    t1, t2 = split(t_ref[0]), split(t_ref[1])
-    v1, v2 = split(vcol[:, :nb]), split(vcol[:, nb:])
-    for p, (t, v) in enumerate(((t1, v1), (t2, v2))):
-        u_high, u_low = split(dot3(t, v, NT))
-        for i in range(8):
-            at = SLOT[p * 8 + i] * sub
-            uh[at:at + sub, :] = u_high[i * sub:(i + 1) * sub, :]
-            ul[at:at + sub, :] = u_low[i * sub:(i + 1) * sub, :]
+    v_ring(3)
+
     for op in gd:
         op.wait_recv()
     ge = go(copy(gfull.at[k, mine], gfull.at[k, mine], x_far))
@@ -331,6 +322,17 @@
     pass_g((0,))
     row_ring(4, pass_row)
     z_ring(4)
+    v_ring(4)
+
+    loads[2].wait()
+    t1, t2 = split(t_ref[0]), split(t_ref[1])
+    v1, v2 = split(vcol[:, :nb]), split(vcol[:, nb:])
+    for p, (t, v) in enumerate(((t1, v1), (t2, v2))):
+        u_high, u_low = split(dot3(t, v, NT))
+        for i in range(8):
+            at = SLOT[p * 8 + i] * sub
+            uh[at:at + sub, :] = u_high[i * sub:(i + 1) * sub, :]
+            ul[at:at + sub, :] = u_low[i * sub:(i + 1) * sub, :]
     yt1 = dot3(t1, split(zcol[:nb, :]), TN)
     yt1_ref[...] = yt1
     qh[:nb, :], ql[:nb, :] = split(yt1)

time: 89.9 us -> 88.2 us (0.981)
  Pallas kernels: 87.4 us -> 85.4 us
    pallas_call x1, Pallas kernels: 87.4 us -> 85.4 us  [body(): pl.pallas_call(kernel, out_shape=jax.ShapeDtypeStruct((rows, cols), F32),...]
where the time goes in v5:
time: 88.2 us; the launch traced here: 87.9 us
  Pallas kernels  85.4 us (97%)
  other arithmetic  2.4 us (3%)
    pallas_call x1, Pallas kernels, body(): pl.pallas_call(kernel, out_shape=jax.ShapeDtypeStruct((rows, cols), F32),...  85.4 us
    add x1, other arithmetic, body(): return matrix + update  2.4 us

profile of v5, /device:TPU:1, one launch (start us, length us, event | category | flops | bytes accessed | tf_op | source)
XLA Modules:
  0.0 87.9 jit_solution(16524609878867929289)
XLA Ops:
  0.0 0.0 copy-start
  0.0 85.4 %two_panels.1 = f32[768,384]{1,0:T(8,128)} custom-call(f32[768,384]{1,0:T(8,128)} %a_hbm.1, f32[768,512]{1,0:T(8,128)} %v_hbm.1, f32[2,256,256]{2,1,0:T(8,128)} %t_hbm.1), custom_call_target="tpu_custom_call" | custom-call | tf_op jit(solution)/shard_map/two_panels/pallas_call | solution.py:419
  85.5 0.0 copy-done
  85.5 2.4 %add.3 = f32[768,384]{1,0:T(8,128)} add(f32[768,384]{1,0:T(8,128)S(1)} %copy-done, f32[768,384]{1,0:T(8,128)} %two_panels.1) | non-fusion elementwise | flops 294912 | bytes 3538944 | tf_op jit(solution)/shard_map/add | solution.py:457
Async XLA Ops:
  0.0 85.5 %copy-start = (f32[768,384]{1,0:T(8,128)S(1)}, f32[768,384]{1,0:T(8,128)}, u32[]{:S(2)}) copy-start(f32[768,384]{1,0:T(8,128)} %a_hbm.1) | copy-start | bytes 3538948
